TPU v7x, 32 devices: a whole 2x2x4 slice. The times are simulated.
32 devices in a mesh: mem: 4 (over y, x), col: 8 (over z, core).
Axes of the slice: x: 2, y: 2, z: 4, core: 2. Of those that a mesh axis runs over, the one named last changes fastest.
Arguments:
- ensemble: bfloat16 [256, 3, 128, 1024], P('mem', None, None, 'col'), may hold values from -6 to 6
- increment: bfloat16 [3, 128, 1024], P(None, 'mem', 'col'), may hold values from -6 to 6
- vert_root: bfloat16 [3, 128, 128], replicated, may hold values from -1 to 2, as said below
- tiles: bfloat16 [8, 8, 128, 128], replicated, may hold values from -2 to 3, as said below
- tile_col: int32 [8, 8], replicated, may hold values from 0 to 7
- level_reach: int32 [128], replicated, may hold values from 2 to 8, as said below
Outputs:
- covaried: bfloat16 [3, 128, 1024], P(None, 'mem', 'col')
Inputs may be any that keep to these rules, and one draw needn't show every extreme that they name: `vert_root`: each variable's matrix is the identity plus bounded noise. `tiles`: slot 0 of block row r is the identity plus bounded noise; the other slots are bounded noise. `level_reach`: level 0 uses 2 slots and the top level uses all 8; the count mostly rises with the level.
All inputs are finite; a program needn't handle non-finite values.
Results may differ from a plain program's by a relative error of at most 0.012.
Values may be sent and summed in bfloat16 or wider, within the bound.
A program may use at most 128 MiB of HBM per device.

v0:
```python
import jax
import jax.numpy as jnp
from jax import lax
from jax.sharding import PartitionSpec as P


def on_device(ensemble, increment, vert_root, tiles, tile_col, level_reach):
    columns_axis = lax.axis_size("col")
    members_all = ensemble.shape[0] * lax.axis_size("mem")
    levels = vert_root.shape[1]
    local_levels = levels // columns_axis
    n_blocks = tiles.shape[0]
    width = tiles.shape[2]
    col_index = lax.axis_index("col")
    whole_incr = lax.all_gather(increment, "mem", axis=1, tiled=True)
    weighted_increment = (
        ensemble.astype(jnp.float32) * whole_incr.astype(jnp.float32)[None]
    ).astype(jnp.bfloat16)
    position = jnp.arange(levels, dtype=jnp.int32)
    within = jnp.arange(local_levels, dtype=jnp.int32)
    mine = col_index * local_levels + within
    sorted_vertical_factor = jnp.take(vert_root, position, axis=2)
    lifted_increment = jnp.einsum(
        "vkq,mvkc->mvqc",
        sorted_vertical_factor,
        weighted_increment,
        preferred_element_type=jnp.float32,
    ).astype(jnp.bfloat16)
    reach_mine = jnp.take(level_reach, mine)
    gathered = lax.all_to_all(lifted_increment, "col", split_axis=2, concat_axis=3, tiled=True)
    items = gathered.shape[0]
    row_count = items * gathered.shape[1]
    planes = gathered.reshape(row_count, local_levels, n_blocks, width)

    def level_step(level, result):
        plane = lax.dynamic_index_in_dim(planes, level, 1, keepdims=False)

        def slot_step(slot, acc):
            sources = lax.dynamic_index_in_dim(tile_col, slot, 1, keepdims=False)
            picked = jnp.take(plane, sources, axis=1)
            blocks = lax.dynamic_index_in_dim(tiles, slot, 1, keepdims=False)
            return acc + jnp.einsum(
                "rbi,bij->rbj", picked, blocks, preferred_element_type=jnp.float32
            )

        summed = lax.fori_loop(
            0, reach_mine[level], slot_step, jnp.zeros((row_count, n_blocks, width), jnp.float32)
        )
        return lax.dynamic_update_index_in_dim(result, summed.astype(jnp.bfloat16), level, 1)

    spread_increment = lax.fori_loop(
        0,
        local_levels,
        level_step,
        jnp.zeros((row_count, local_levels, n_blocks, width), jnp.bfloat16),
    )
    spread_increment = spread_increment.reshape(gathered.shape)
    returned_increment = lax.all_to_all(
        spread_increment, "col", split_axis=3, concat_axis=2, tiled=True
    )
    lowered_increment = jnp.einsum(
        "vlq,mvqc->mvlc",
        sorted_vertical_factor,
        returned_increment,
        preferred_element_type=jnp.float32,
    )
    partial_sum = jnp.sum(ensemble.astype(jnp.float32) * lowered_increment, axis=0)
    summed_all = lax.psum(partial_sum.astype(jnp.bfloat16), "mem").astype(jnp.float32)
    group_levels = levels // lax.axis_size("mem")
    share = lax.dynamic_slice_in_dim(
        summed_all, lax.axis_index("mem") * group_levels, group_levels, 1
    )
    return (share / (members_all - 1)).astype(jnp.bfloat16)


def solution(mesh):
    placed = (P("mem", None, None, "col"), P(None, "mem", "col"), P(), P(), P(), P())
    return jax.shard_map(
        on_device, mesh=mesh, in_specs=placed, out_specs=P(None, "mem", "col"), check_vma=False
    )
```

profile of v0, /device:TPU:0, one launch (start us, length us, event | category | flops | bytes accessed | tf_op | source)
XLA Modules:
  0.0 820.4 jit_solution(9028172028955095301)
XLA Ops:
  6.6 8.7 %copy.57 = bf16[64,3,128,128]{2,3,0,1:T(8,128)(2,1)} copy(bf16[64,3,128,128]{3,2,1,0:T(8,128)(2,1)} %param.10) | data formatting | bytes 12582912 | tf_op args[0]
  16.5 9.8 %all_gather.3 = bf16[3,128,128]{2,1,0:T(8,128)(2,1)S(1)} all-gather(bf16[3,32,128]{2,1,0:T(8,128)(2,1)S(1)} %copy-done.4), channel_id=1, replica_groups=mesh['mem'=4,'col'=8] {'mem'}, dimensions={1}, use_global_device_ids=true | all-gather | bytes 122880 | tf_op jit(solution)/shard_map/all_gather | solution.py:15
  26.4 7.3 convert_bitcast_fusion.1
  33.7 9.1 %copy.61 = bf16[64,3,128,128]{3,0,1,2:T(8,128)(2,1)} copy(bf16[64,3,128,128]{2,3,0,1:T(8,128)(2,1)} %convert_bitcast_fusion.1) | data formatting | bytes 12582912 | tf_op jit(solution)/shard_map/convert_element_type | solution.py:28
  42.8 5.0 all-to-all-start
  48.0 1.5 copy.64
  50.3 136.5 %all-to-all-done = bf16[64,3,128,128]{3,0,1,2:T(8,128)(2,1)} async-done(((bf16[64,3,128,128]{3,0,1,2:T(8,128)(2,1)}), bf16[64,3,128,128]{3,0,1,2:T(8,128)(2,1)}, u32[]{:S(2)}, u32[]{:S(2)}) %all-to-all-start) | async-done | bytes 6291488 | tf_op jit(solution)/shard_map/all_to_all | solution.py:30
  186.8 6.8 copy.62
  193.7 6.7 copy.63
  200.4 141.4 %while.36 = (s32[]{:T(128)}, bf16[192,16,8,128]{3,2,1,0:T(8,128)(2,1)}, s32[16]{0:T(128)S(1)}, bf16[192,16,8,128]{3,0,2,1:T(8,128)(2,1)}, bf16[8,8,128,128]{3,2,...) while((s32[]{:T(128)}, ...), condition=%wide.region_3.4_spmd, body=%wide.region_0.3_spmd.sunk | while | flops 50922548 | bytes 6558704 | solution.py:51
  202.1 6.0 while.37
  206.1 1.4 fusion.28
  210.9 6.0 while.37
  212.2 1.4 fusion.28
  219.7 6.0 while.37
  221.0 1.4 fusion.28
  223.7 1.4 fusion.28
  228.6 6.0 while.37
  232.6 1.4 fusion.28
  237.4 6.0 while.37
  238.7 1.4 fusion.28
  246.3 6.0 while.37
  247.6 1.4 fusion.28
  255.1 6.0 while.37
  263.9 6.0 while.37
  265.3 1.4 fusion.28
  267.9 1.4 fusion.28
  272.8 6.0 while.37
  281.6 6.0 while.37
  282.9 1.4 fusion.28
  290.4 6.0 while.37
  294.4 1.4 fusion.28
  299.3 6.0 while.37
  303.3 1.4 fusion.28
  308.1 6.0 while.37
  312.1 1.4 fusion.28
  317.0 6.0 while.37
  325.8 6.0 while.37
  329.8 1.4 fusion.28
  334.7 6.0 while.37
  341.8 10.4 %reshape.38 = bf16[64,3,16,1024]{3,2,1,0:T(8,128)(2,1)} reshape(bf16[192,16,8,128]{3,2,1,0:T(8,128)(2,1)} %get-tuple-element.147) | data formatting | bytes 12582912 | tf_op jit(solution)/shard_map/reshape | solution.py:57
  352.2 20.7 %copy.67 = bf16[64,3,16,1024]{0,2,1,3:T(8,128)(2,1)} copy(bf16[64,3,16,1024]{3,2,1,0:T(8,128)(2,1)} %reshape.38) | data formatting | bytes 12582912 | tf_op jit(solution)/shard_map/reshape | solution.py:57
  372.9 13.8 %reshape.65 = bf16[8,2,196608]{2,1,0:T(2,128)(2,1)} reshape(bf16[1024,3,16,64]{3,2,1,0:T(8,128)(2,1)} %bitcast.61) | data formatting | bytes 12582912
  386.7 345.5 %all_to_all.33 = bf16[8,2,196608]{2,1,0:T(2,128)(2,1)} all-to-all(bf16[8,2,196608]{2,1,0:T(2,128)(2,1)} %reshape.65), channel_id=1, replica_groups=mesh['mem'=4,'col'=8] {'col'}, dimensions={0} | all-to-all | bytes 12582912 | tf_op jit(solution)/shard_map/all_to_all | solution.py:58
  732.2 13.3 %reshape.66 = bf16[1024,3,16,64]{3,2,1,0:T(8,128)(2,1)} reshape(bf16[8,2,196608]{2,1,0:T(2,128)(2,1)} %all_to_all.33) | data formatting | bytes 12582912
  745.5 18.5 %copy.69 = bf16[64,3,8,16,128]{4,3,2,1,0:T(8,128)(2,1)} copy(bf16[64,3,8,16,128]{0,3,1,4,2:T(8,128)(2,1)} %bitcast.62) | data formatting | bytes 12582912 | tf_op jit(solution)/shard_map/all_to_all | solution.py:58
  764.0 7.5 fusion.10
  772.2 40.0 %all-reduce.2.cloned.1.call-done = bf16[3,128,128]{2,1,0:T(8,128)(2,1)} async-done(((bf16[3,128,128]{2,1,0:T(8,128)(2,1)}), bf16[3,128,128]{2,1,0:T(8,128)(2,1)}) %all-reduce.2.cloned.1.call-update) | async-done | bytes 98320 | tf_op jit(solution)/shard_map/psum | solution.py:68
  (224 shorter events, 94.5 us)
Async XLA Ops:
  6.5 43.1 %copy-start = (s32[128]{0:T(128)S(1)}, s32[128]{0:T(128)}, u32[]{:S(2)}) copy-start(s32[128]{0:T(128)} %param.15) | copy-start | bytes 1540
  6.5 8.7 %copy-start.3 = (bf16[3,128,128]{2,1,0:T(8,128)(2,1)S(1)}, bf16[3,128,128]{2,1,0:T(8,128)(2,1)}, u32[]{:S(2)}) copy-start(bf16[3,128,128]{2,1,0:T(8,128)(2,1)} %param.12) | copy-start | bytes 294916
  6.5 9.9 %copy-start.4 = (bf16[3,32,128]{2,1,0:T(8,128)(2,1)S(1)}, bf16[3,32,128]{2,1,0:T(8,128)(2,1)}, u32[]{:S(2)}) copy-start(bf16[3,32,128]{2,1,0:T(8,128)(2,1)} %param.11) | copy-start | bytes 73732
  42.8 5.2 copy-start.2
  42.8 6.7 copy-start.5
  42.8 144.0 %all-to-all-start = ((bf16[64,3,128,128]{3,0,1,2:T(8,128)(2,1)}), bf16[64,3,128,128]{3,0,1,2:T(8,128)(2,1)}, u32[]{:S(2)}, u32[]{:S(2)}) async-start(bf16[64,3,128,128]{3,0,1,2:T(8,128)(2,1)} %copy.61), calls=%async_computation | async-start | bytes 12582912 | tf_op jit(solution)/shard_map/all_to_all | solution.py:30
  47.8 764.5 %all-reduce.2.cloned.1.call-start = ((), (), s32[]{:S(2)}) async-start(), calls=%async_computation.2 | async-start | bytes 196608 | tf_op jit(solution)/shard_map/psum | solution.py:68
  764.0 49.6 %copy-start.1 = (s32[128]{0:T(128)S(1)}, s32[128]{0:T(128)}, u32[]{:S(2)}) copy-start(s32[128]{0:T(128)} %param.15) | copy-start | bytes 1540
Sparse Core Ops, SparseCore 0:
  772.4 39.8 all-reduce.1
where the time goes:
time: 823 us; the launch traced here: 820 us
  blocking collectives  355 us (43%)
  waiting for transfers between devices  177 us (22%)
  local copies, waits for them, and re-layouts  176 us (21%)
  matrix products  58.5 us (7%)
  loops' own time  32.2 us (4%)
  between operations  13.5 us (2%)
    all_to_all x1, blocking collectives, on_device(): lax.all_to_all(spread_increment, 'col', split_axis=3, concat_axis=2, tile...  346 us
    all_to_all x1, waiting for transfers between devices, on_device(): lax.all_to_all(lifted_increment, 'col', split_axis=2, concat_axis=3, tile...  137 us
    dot_general x32, matrix products, slot_step(): jnp.einsum('rbi,bij->rbj', picked, blocks, preferred_element_type=jnp.flo...  43.8 us
    psum x1, waiting for transfers between devices, on_device(): lax.psum(partial_sum.astype(jnp.bfloat16), 'mem').astype(jnp.float32)  40 us
    unnamed x16, local copies, waits for them, and re-layouts  35.9 us
    another operation x16, loops' own time, level_step(): lax.fori_loop(0, reach_mine[level], slot_step, jnp.zeros((row_count, n_bl...  31.8 us
    reshape x2, local copies, waits for them, and re-layouts, on_device(): spread_increment = spread_increment.reshape(gathered.shape)  31.1 us
    gather x32, local copies, waits for them, and re-layouts, slot_step(): picked = jnp.take(plane, sources, axis=1)  20 us
  transfers between devices with their start and end apart: 2, of which 2 were waited for; matrix products, arithmetic and copies ran while one was open for 0% of the time, Pallas kernels for 0%

commit v1 on v0

v1 whole, which is shorter than its diff:
```python
import functools

import jax
import jax.numpy as jnp
from jax import lax
from jax.experimental import pallas as pl
from jax.experimental.pallas import tpu as pltpu
from jax.sharding import PartitionSpec as P


def kernel(
    n_mem, n_col, halves, scale,
    slot_block, ens, inc, root, root_t, tiles, active, out,
    recv, incr, grid, picked, total, part_out, part_in, line_out, line_in,
    send_sem, recv_sem, own_sem, inc_send, inc_recv, inc2_send, inc2_recv,
    part_send, part_recv, line_send, line_recv,
):
    mem, col = lax.axis_index("mem"), lax.axis_index("col")
    variables, levels, width = ens.shape[1], ens.shape[2], ens.shape[3]
    per_device = ens.shape[0] // n_col
    group = per_device // halves
    quarter = levels // n_mem
    slots = active.shape[0]
    chunks = variables * halves

    def col_peer(step):
        return lax.rem(col + step, n_col)

    def mem_peer(step):
        return lax.rem(mem + step, n_mem)

    def each(low, high, body):
        def step(index, carry):
            body(index)
            return carry
        lax.fori_loop(low, high, step, 0)

    def remote(src, dst, send, receive, peer):
        return pltpu.make_async_remote_copy(
            src_ref=src, dst_ref=dst, send_sem=send, recv_sem=receive,
            device_id=peer, device_id_type=pl.DeviceIdType.MESH,
        )

    def members_of(owner, chunk):
        first = owner * per_device + lax.rem(chunk, halves) * group
        return ens.at[pl.ds(first, group), chunk // halves]

    def member_copy(chunk, step):
        peer = col_peer(step)
        return remote(
            members_of(peer, chunk), recv.at[chunk, col],
            send_sem.at[chunk, peer], recv_sem.at[chunk, col], {"col": peer},
        )

    def member_arrival(chunk, step):
        peer = col_peer(step)
        return remote(
            members_of(peer, chunk), recv.at[chunk, peer],
            send_sem.at[chunk, peer], recv_sem.at[chunk, peer], {"col": peer},
        )

    def own_copy(chunk):
        return pltpu.make_async_copy(
            members_of(col, chunk), recv.at[chunk, col], own_sem.at[chunk]
        )

    def send_chunk(chunk):
        own_copy(chunk).start()
        each(1, n_col, lambda step: member_copy(chunk, step).start())

    def inc_copy(step):
        peer = col_peer(step)
        return remote(inc, incr.at[mem, col], inc_send.at[peer], inc_recv.at[col], {"col": peer})

    def inc_arrival(step):
        peer = col_peer(step)
        return remote(inc, incr.at[mem, peer], inc_send.at[peer], inc_recv.at[peer], {"col": peer})

    def inc2_copy(step):
        peer = mem_peer(step)
        return remote(
            incr.at[mem], incr.at[mem], inc2_send.at[peer], inc2_recv.at[mem], {"mem": peer}
        )

    def inc2_arrival(step):
        peer = mem_peer(step)
        return remote(
            incr.at[peer], incr.at[peer], inc2_send.at[peer], inc2_recv.at[peer], {"mem": peer}
        )

    def part_copy(v, step):
        peer = mem_peer(step)
        return remote(
            part_out.at[v, peer], part_in.at[v, mem],
            part_send.at[v, peer], part_recv.at[v, mem], {"mem": peer},
        )

    def part_arrival(v, step):
        peer = mem_peer(step)
        return remote(
            part_out.at[v, peer], part_in.at[v, peer],
            part_send.at[v, peer], part_recv.at[v, peer], {"mem": peer},
        )

    def line_copy(v, step):
        peer = col_peer(step)
        return remote(
            line_out.at[v, peer], line_in.at[v, col],
            line_send.at[v, peer], line_recv.at[v, col], {"col": peer},
        )

    def line_arrival(v, step):
        peer = col_peer(step)
        return remote(
            line_out.at[v, peer], line_in.at[v, peer],
            line_send.at[v, peer], line_recv.at[v, peer], {"col": peer},
        )

    barrier = pltpu.get_barrier_semaphore()
    for step in range(1, n_col):
        pl.semaphore_signal(
            barrier, inc=1, device_id={"col": col_peer(step)},
            device_id_type=pl.DeviceIdType.MESH,
        )
    for step in range(1, n_mem):
        pl.semaphore_signal(
            barrier, inc=1, device_id={"mem": mem_peer(step)},
            device_id_type=pl.DeviceIdType.MESH,
        )
    pl.semaphore_wait(barrier, n_col + n_mem - 2)

    each(1, n_col, lambda step: inc_copy(step).start())
    send_chunk(0)
    if chunks > 1:
        send_chunk(1)
    incr[mem, col] = inc[...]
    each(1, n_col, lambda step: inc_arrival(step).wait_recv())
    each(1, n_mem, lambda step: inc2_copy(step).start())
    each(1, n_mem, lambda step: inc2_arrival(step).wait_recv())

    def finish_levels(v):
        each(1, n_mem, lambda step: part_arrival(v, step).wait_recv())

        def block(b):
            summed = total[v, mem, b]
            for step in range(1, n_mem):
                summed += part_in[v, mem_peer(step), b].astype(jnp.float32)
            total[v, mem, b] = summed
            line_out[v, b] = summed.astype(jnp.bfloat16)

        each(0, n_col, block)
        each(1, n_col, lambda step: line_copy(v, step).start())

    def chunk_step(chunk):
        v, half = chunk // halves, lax.rem(chunk, halves)
        own_copy(chunk).wait()
        each(1, n_col, lambda step: member_arrival(chunk, step).wait_recv())

        @pl.when(chunk + 2 < chunks)
        def _():
            send_chunk(chunk + 2)

        def lift(b):
            field = jnp.concatenate([incr[p, b, v] for p in range(n_mem)], 0).astype(jnp.float32)
            weighted = jnp.concatenate(
                [
                    (recv[chunk, b, i].astype(jnp.float32) * field).astype(jnp.bfloat16)
                    for i in range(group)
                ],
                1,
            )
            lifted = jnp.dot(
                root_t[v], weighted, preferred_element_type=jnp.float32
            ).astype(jnp.bfloat16)
            for i in range(group):
                grid[b, i] = lifted[:, i * width:(i + 1) * width]

        each(0, n_col, lift)

        def spread(r):
            for s in range(slots):
                source = grid[slot_block[r, s]]
                picked[:, :, s * width:(s + 1) * width] = source * active[s][None]
            spread_rows = jnp.dot(
                picked[...].reshape(group * levels, slots * width), tiles[r],
                preferred_element_type=jnp.float32,
            ).astype(jnp.bfloat16)
            side = jnp.concatenate(
                [spread_rows[i * levels:(i + 1) * levels] for i in range(group)], 1
            )
            lowered = jnp.dot(root[v], side, preferred_element_type=jnp.float32)
            summed = recv[chunk, r, 0].astype(jnp.float32) * lowered[:, :width]
            for i in range(1, group):
                summed += (
                    recv[chunk, r, i].astype(jnp.float32) * lowered[:, i * width:(i + 1) * width]
                )
            for p in range(n_mem):
                piece = summed[p * quarter:(p + 1) * quarter]

                @pl.when(half == 0)
                def _():
                    total[v, p, r] = piece

                @pl.when(half != 0)
                def _():
                    total[v, p, r] += piece

                @pl.when(half == halves - 1)
                def _():
                    part_out[v, p, r] = total[v, p, r].astype(jnp.bfloat16)

        each(0, n_col, spread)

        @pl.when(half == halves - 1)
        def _():
            each(1, n_mem, lambda step: part_copy(v, step).start())

        @pl.when((half == 0) & (v > 0))
        def _():
            finish_levels(v - 1)

    each(0, chunks, chunk_step)
    finish_levels(variables - 1)

    for v in range(variables):
        each(1, n_col, lambda step: line_arrival(v, step).wait_recv())
        summed = total[v, mem, col]
        for step in range(1, n_col):
            summed += line_in[v, col_peer(step)].astype(jnp.float32)
        out[v] = (summed / scale).astype(out.dtype)

    each(1, n_col, lambda step: inc_copy(step).wait_send())
    each(1, n_mem, lambda step: inc2_copy(step).wait_send())
    each(0, chunks, lambda chunk: each(
        1, n_col, lambda step: member_copy(chunk, step).wait_send()))
    each(0, variables, lambda v: each(
        1, n_mem, lambda step: part_copy(v, step).wait_send()))
    each(0, variables, lambda v: each(
        1, n_col, lambda step: line_copy(v, step).wait_send()))


def on_device(ensemble, increment, vert_root, tiles, tile_col, level_reach):
    n_mem, n_col = lax.axis_size("mem"), lax.axis_size("col")
    members, variables, levels, width = ensemble.shape
    n_blocks, slots = tiles.shape[:2]
    per_device = members // n_col
    halves = 2 if per_device % 2 == 0 else 1
    group = per_device // halves
    chunks = variables * halves
    quarter = levels // n_mem
    active = jnp.broadcast_to(
        (jnp.arange(slots, dtype=jnp.int32)[:, None] < level_reach[None])[:, :, None],
        (slots, levels, width),
    ).astype(jnp.bfloat16)
    dma = pltpu.SemaphoreType.DMA
    vmem = pl.BlockSpec(memory_space=pltpu.VMEM)
    bf16 = jnp.bfloat16
    return pl.pallas_call(
        functools.partial(kernel, n_mem, n_col, halves, float(members * n_mem - 1)),
        out_shape=jax.ShapeDtypeStruct(increment.shape, bf16),
        in_specs=[
            pl.BlockSpec(memory_space=pltpu.SMEM),
            pl.BlockSpec(memory_space=pl.ANY),
            vmem, vmem, vmem, vmem, vmem,
        ],
        out_specs=vmem,
        scratch_shapes=[
            pltpu.VMEM((chunks, n_col, group, levels, width), bf16),
            pltpu.VMEM((n_mem, n_col, variables, quarter, width), bf16),
            pltpu.VMEM((n_col, group, levels, width), bf16),
            pltpu.VMEM((group, levels, slots * width), bf16),
            pltpu.VMEM((variables, n_mem, n_col, quarter, width), jnp.float32),
            pltpu.VMEM((variables, n_mem, n_col, quarter, width), bf16),
            pltpu.VMEM((variables, n_mem, n_col, quarter, width), bf16),
            pltpu.VMEM((variables, n_col, quarter, width), bf16),
            pltpu.VMEM((variables, n_col, quarter, width), bf16),
            dma((chunks, n_col)),
            dma((chunks, n_col)),
            dma((chunks,)),
            dma((n_col,)),
            dma((n_col,)),
            dma((n_mem,)),
            dma((n_mem,)),
            dma((variables, n_mem)),
            dma((variables, n_mem)),
            dma((variables, n_col)),
            dma((variables, n_col)),
        ],
        compiler_params=pltpu.CompilerParams(
            collective_id=0, has_side_effects=True, vmem_limit_bytes=56 * 1024 * 1024
        ),
        name="localized_covariance",
    )(
        tile_col, ensemble, increment, vert_root, jnp.swapaxes(vert_root, 1, 2),
        tiles.reshape(n_blocks, slots * width, width), active,
    )


def solution(mesh):
    placed = (P("mem", None, None, "col"), P(None, "mem", "col"), P(), P(), P(), P())
    return jax.shard_map(
        on_device, mesh=mesh, in_specs=placed, out_specs=P(None, "mem", "col"), check_vma=False
    )
```

time: 823 us -> 173 us (0.21)
  blocking collectives: 355 us -> 0 us
  waiting for transfers between devices: 177 us -> 0 us
  local copies, waits for them, and re-layouts: 176 us -> 3.88 us
  Pallas kernels: 0 us -> 168 us
  matrix products: 58.5 us -> 0 us
  loops' own time: 32.2 us -> 0 us
  between operations: 13.5 us -> 0.01 us
    all_to_all x1 -> x0, blocking collectives: 346 us -> none  [on_device(): lax.all_to_all(spread_increment, 'col', split_axis=3, concat_axis=2, tile...]
    pallas_call x0 -> x1, Pallas kernels: none -> 168 us  [on_device(): pl.pallas_call(functools.partial(kernel, n_mem, n_col, halves, float(memb...]
    all_to_all x1 -> x0, waiting for transfers between devices: 137 us -> none  [on_device(): lax.all_to_all(lifted_increment, 'col', split_axis=2, concat_axis=3, tile...]
    dot_general x34 -> x0, matrix products: 58.5 us -> none  [the longest x32 43.8 us: slot_step(): jnp.einsum('rbi,bij->rbj', picked, blocks, preferred_element_type=jnp.flo...]
    psum x1 -> x0, waiting for transfers between devices: 40 us -> none  [on_device(): lax.psum(partial_sum.astype(jnp.bfloat16), 'mem').astype(jnp.float32)]
    unnamed x16 -> x2, local copies, waits for them, and re-layouts: 35.9 us -> 2.98 us
    another operation x17 -> x0, loops' own time: 32.2 us -> none  [the longest x16 31.8 us: level_step(): lax.fori_loop(0, reach_mine[level], slot_step, jnp.zeros((row_count, n_bl...]
    reshape x2 -> x0, local copies, waits for them, and re-layouts: 31.1 us -> none  [on_device(): spread_increment = spread_increment.reshape(gathered.shape)]
  transfers between devices with their start and end apart: 2 -> 0, of which waited for: 2 -> 0; matrix products, arithmetic and copies ran while one was open for 0% -> 0% of each run, Pallas kernels for 0% -> 0%
where the time goes in v1:
time: 173 us
  Pallas kernels  168 us (97%)
  local copies, waits for them, and re-layouts  3.88 us (2%)
    pallas_call x1, Pallas kernels, on_device(): pl.pallas_call(functools.partial(kernel, n_mem, n_col, halves, float(memb...  168 us

profile of v1, /device:TPU:0, one launch (start us, length us, event | category | flops | bytes accessed | tf_op | source)
XLA Modules:
  0.0 172.6 jit_solution(11366663106200958422)
XLA Ops:
  0.0 0.7 fusion
  0.7 1.6 copy.7
  2.3 0.9 broadcast_in_dim.2.active
  3.2 168.1 %localized_covariance.1 = bf16[3,32,128]{2,1,0:T(8,128)(2,1)} custom-call(s32[8,8]{1,0:T(8,128)} %slot_block.1, bf16[64,3,128,128]{3,2,1,0:T(8,128)(2,1)} %ens.1, bf16[3,32,128]{2,1,0:T(8,128)(2,1)} %inc.1, bf16[3,128,128]{2,1,0:T(8,128)(2,1)} %root.1, bf16[3,128,128]{2,1,0:T(8,128)(2,1)} %bitcast.3, bf16[8,1024,128]{2,1,0:T(8,128)(2,1)} %bitcast.2, ...), custom_call_target="tpu_custom_call" | custom-call | tf_op jit(solution)/shard_map/localized_covariance/pallas_call | solution.py:258
  171.3 1.3 copy.9

commit v2 on v1

--- a/solution.py
+++ b/solution.py
@@ -10,8 +10,8 @@
 
 def kernel(
     n_mem, n_col, halves, scale,
-    slot_block, ens, inc, root, root_t, tiles, active, out,
-    recv, incr, grid, picked, total, part_out, part_in, line_out, line_in,
+    slot_block, ens, inc, root_in, tiles_in, reach, out,
+    root, root_t, tiles, active, load_sem, recv, incr, grid, picked, total, part_out, part_in, line_out, line_in,
     send_sem, recv_sem, own_sem, inc_send, inc_recv, inc2_send, inc2_recv,
     part_send, part_recv, line_send, line_recv,
 ):
@@ -22,6 +22,7 @@
     quarter = levels // n_mem
     slots = active.shape[0]
     chunks = variables * halves
+    ahead = min(4, chunks)
 
     def col_peer(step):
         return lax.rem(col + step, n_col)
@@ -116,6 +117,11 @@
             line_send.at[v, peer], line_recv.at[v, peer], {"col": peer},
         )
 
+    root_load = pltpu.make_async_copy(root_in, root, load_sem.at[0])
+    tiles_load = pltpu.make_async_copy(tiles_in, tiles, load_sem.at[1])
+    root_load.start()
+    tiles_load.start()
+
     barrier = pltpu.get_barrier_semaphore()
     for step in range(1, n_col):
         pl.semaphore_signal(
@@ -130,10 +136,21 @@
     pl.semaphore_wait(barrier, n_col + n_mem - 2)
 
     each(1, n_col, lambda step: inc_copy(step).start())
-    send_chunk(0)
-    if chunks > 1:
-        send_chunk(1)
+    each(0, ahead, send_chunk)
     incr[mem, col] = inc[...]
+    reach_rows = jnp.broadcast_to(reach[...].astype(jnp.float32), (width, levels)).T
+    for s in range(slots):
+        active[s] = jnp.where(reach_rows > float(s), 1.0, 0.0).astype(jnp.bfloat16)
+    root_load.wait()
+    for v in range(variables):
+        root_t[v] = root[v].astype(jnp.float32).T.astype(jnp.bfloat16)
+
+    def clear(v):
+        for p in range(n_mem):
+            total[v, p] = jnp.zeros(total.shape[2:], jnp.float32)
+
+    each(0, variables, clear)
+    tiles_load.wait()
     each(1, n_col, lambda step: inc_arrival(step).wait_recv())
     each(1, n_mem, lambda step: inc2_copy(step).start())
     each(1, n_mem, lambda step: inc2_arrival(step).wait_recv())
@@ -156,9 +173,9 @@
         own_copy(chunk).wait()
         each(1, n_col, lambda step: member_arrival(chunk, step).wait_recv())
 
-        @pl.when(chunk + 2 < chunks)
+        @pl.when(chunk + ahead < chunks)
         def _():
-            send_chunk(chunk + 2)
+            send_chunk(chunk + ahead)
 
         def lift(b):
             field = jnp.concatenate([incr[p, b, v] for p in range(n_mem)], 0).astype(jnp.float32)
@@ -195,18 +212,11 @@
                     recv[chunk, r, i].astype(jnp.float32) * lowered[:, i * width:(i + 1) * width]
                 )
             for p in range(n_mem):
-                piece = summed[p * quarter:(p + 1) * quarter]
-
-                @pl.when(half == 0)
-                def _():
-                    total[v, p, r] = piece
-
-                @pl.when(half != 0)
-                def _():
-                    total[v, p, r] += piece
-
-                @pl.when(half == halves - 1)
-                def _():
+                total[v, p, r] += summed[p * quarter:(p + 1) * quarter]
+
+            @pl.when(half == halves - 1)
+            def _():
+                for p in range(n_mem):
                     part_out[v, p, r] = total[v, p, r].astype(jnp.bfloat16)
 
         each(0, n_col, spread)
@@ -244,14 +254,10 @@
     members, variables, levels, width = ensemble.shape
     n_blocks, slots = tiles.shape[:2]
     per_device = members // n_col
-    halves = 2 if per_device % 2 == 0 else 1
+    halves = per_device // 2 if per_device % 4 == 0 else 2 - per_device % 2
     group = per_device // halves
     chunks = variables * halves
     quarter = levels // n_mem
-    active = jnp.broadcast_to(
-        (jnp.arange(slots, dtype=jnp.int32)[:, None] < level_reach[None])[:, :, None],
-        (slots, levels, width),
-    ).astype(jnp.bfloat16)
     dma = pltpu.SemaphoreType.DMA
     vmem = pl.BlockSpec(memory_space=pltpu.VMEM)
     bf16 = jnp.bfloat16
@@ -261,10 +267,15 @@
         in_specs=[
             pl.BlockSpec(memory_space=pltpu.SMEM),
             pl.BlockSpec(memory_space=pl.ANY),
-            vmem, vmem, vmem, vmem, vmem,
+            vmem, pl.BlockSpec(memory_space=pl.ANY), pl.BlockSpec(memory_space=pl.ANY), vmem,
         ],
         out_specs=vmem,
         scratch_shapes=[
+            pltpu.VMEM(vert_root.shape, bf16),
+            pltpu.VMEM(vert_root.shape, bf16),
+            pltpu.VMEM((n_blocks, slots * width, width), bf16),
+            pltpu.VMEM((slots, levels, width), bf16),
+            dma((2,)),
             pltpu.VMEM((chunks, n_col, group, levels, width), bf16),
             pltpu.VMEM((n_mem, n_col, variables, quarter, width), bf16),
             pltpu.VMEM((n_col, group, levels, width), bf16),
@@ -291,8 +302,8 @@
         ),
         name="localized_covariance",
     )(
-        tile_col, ensemble, increment, vert_root, jnp.swapaxes(vert_root, 1, 2),
-        tiles.reshape(n_blocks, slots * width, width), active,
+        tile_col, ensemble, increment, vert_root,
+        tiles.reshape(n_blocks, slots * width, width), level_reach.reshape(1, levels),
     )
 
 

time: 173 us -> 169 us (0.977)
  local copies, waits for them, and re-layouts: 3.88 us -> 1.35 us
where the time goes in v2:
time: 169 us
  Pallas kernels  168 us (99%)
    pallas_call x1, Pallas kernels, on_device(): pl.pallas_call(functools.partial(kernel, n_mem, n_col, halves, float(memb...  168 us

profile of v2, /device:TPU:0, one launch (start us, length us, event | category | flops | bytes accessed | tf_op | source)
XLA Modules:
  0.0 169.2 jit_solution(10447284002776775772)
XLA Ops:
  0.0 167.9 %localized_covariance.1 = bf16[3,32,128]{2,1,0:T(8,128)(2,1)} custom-call(s32[8,8]{1,0:T(8,128)} %slot_block.1, bf16[64,3,128,128]{3,2,1,0:T(8,128)(2,1)} %ens.1, bf16[3,32,128]{2,1,0:T(8,128)(2,1)} %inc.1, bf16[3,128,128]{2,1,0:T(8,128)(2,1)} %root_in.1, bf16[8,1024,128]{2,1,0:T(8,128)(2,1)} %bitcast.2, s32[1,128]{1,0:T(1,128)} %bitcast.3), custom_call_target="tpu_custom_call" | custom-call | tf_op jit(solution)/shard_map/localized_covariance/pallas_call | solution.py:264
  167.9 1.3 copy.8

commit v3 on v2

--- a/solution.py
+++ b/solution.py
@@ -11,7 +11,7 @@
 def kernel(
     n_mem, n_col, halves, scale,
     slot_block, ens, inc, root_in, tiles_in, reach, out,
-    root, root_t, tiles, active, load_sem, recv, incr, grid, picked, total, part_out, part_in, line_out, line_in,
+    root, root_t, tiles, active, load_sem, recv, incr, grid, total, part_out, part_in, line_out, line_in,
     send_sem, recv_sem, own_sem, inc_send, inc_recv, inc2_send, inc2_recv,
     part_send, part_recv, line_send, line_recv,
 ):
@@ -22,7 +22,8 @@
     quarter = levels // n_mem
     slots = active.shape[0]
     chunks = variables * halves
-    ahead = min(4, chunks)
+    ahead = min(3, chunks)
+    side_by_side = 4 if n_col % 4 == 0 else 1
 
     def col_peer(step):
         return lax.rem(col + step, n_col)
@@ -36,12 +37,21 @@
             return carry
         lax.fori_loop(low, high, step, 0)
 
+    def together(body):
+        def step(index):
+            for k in range(side_by_side):
+                body(index * side_by_side + k)
+        each(0, n_col // side_by_side, step)
+
     def remote(src, dst, send, receive, peer):
         return pltpu.make_async_remote_copy(
             src_ref=src, dst_ref=dst, send_sem=send, recv_sem=receive,
             device_id=peer, device_id_type=pl.DeviceIdType.MESH,
         )
 
+    def far_first(k):
+        return n_col // 2 + (k // 2) * (1 - 2 * lax.rem(k, 2))
+
     def members_of(owner, chunk):
         first = owner * per_device + lax.rem(chunk, halves) * group
         return ens.at[pl.ds(first, group), chunk // halves]
@@ -67,7 +77,7 @@
 
     def send_chunk(chunk):
         own_copy(chunk).start()
-        each(1, n_col, lambda step: member_copy(chunk, step).start())
+        each(1, n_col, lambda k: member_copy(chunk, far_first(k)).start())
 
     def inc_copy(step):
         peer = col_peer(step)
@@ -192,14 +202,14 @@
             for i in range(group):
                 grid[b, i] = lifted[:, i * width:(i + 1) * width]
 
-        each(0, n_col, lift)
+        together(lift)
 
         def spread(r):
-            for s in range(slots):
-                source = grid[slot_block[r, s]]
-                picked[:, :, s * width:(s + 1) * width] = source * active[s][None]
+            picked = jnp.concatenate(
+                [grid[slot_block[r, s]] * active[s][None] for s in range(slots)], 2
+            )
             spread_rows = jnp.dot(
-                picked[...].reshape(group * levels, slots * width), tiles[r],
+                picked.reshape(group * levels, slots * width), tiles[r],
                 preferred_element_type=jnp.float32,
             ).astype(jnp.bfloat16)
             side = jnp.concatenate(
@@ -214,15 +224,12 @@
             for p in range(n_mem):
                 total[v, p, r] += summed[p * quarter:(p + 1) * quarter]
 
-            @pl.when(half == halves - 1)
-            def _():
-                for p in range(n_mem):
-                    part_out[v, p, r] = total[v, p, r].astype(jnp.bfloat16)
-
-        each(0, n_col, spread)
+        together(spread)
 
         @pl.when(half == halves - 1)
         def _():
+            for p in range(n_mem):
+                part_out[v, p] = total[v, p].astype(jnp.bfloat16)
             each(1, n_mem, lambda step: part_copy(v, step).start())
 
         @pl.when((half == 0) & (v > 0))
@@ -279,7 +286,6 @@
             pltpu.VMEM((chunks, n_col, group, levels, width), bf16),
             pltpu.VMEM((n_mem, n_col, variables, quarter, width), bf16),
             pltpu.VMEM((n_col, group, levels, width), bf16),
-            pltpu.VMEM((group, levels, slots * width), bf16),
             pltpu.VMEM((variables, n_mem, n_col, quarter, width), jnp.float32),
             pltpu.VMEM((variables, n_mem, n_col, quarter, width), bf16),
             pltpu.VMEM((variables, n_mem, n_col, quarter, width), bf16),

time: 169 us -> 166 us (0.982)
  Pallas kernels: 168 us -> 165 us
    pallas_call x1, Pallas kernels: 168 us -> 165 us  [on_device(): pl.pallas_call(functools.partial(kernel, n_mem, n_col, halves, float(memb...]
where the time goes in v3:
time: 166 us
  Pallas kernels  165 us (99%)
    pallas_call x1, Pallas kernels, on_device(): pl.pallas_call(functools.partial(kernel, n_mem, n_col, halves, float(memb...  165 us

profile of v3, /device:TPU:0, one launch (start us, length us, event | category | flops | bytes accessed | tf_op | source)
XLA Modules:
  0.0 166.1 jit_solution(14703537543747507431)
XLA Ops:
  0.0 164.7 %localized_covariance.1 = bf16[3,32,128]{2,1,0:T(8,128)(2,1)} custom-call(s32[8,8]{1,0:T(8,128)} %slot_block.1, bf16[64,3,128,128]{3,2,1,0:T(8,128)(2,1)} %ens.1, bf16[3,32,128]{2,1,0:T(8,128)(2,1)} %inc.1, bf16[3,128,128]{2,1,0:T(8,128)(2,1)} %root_in.1, bf16[8,1024,128]{2,1,0:T(8,128)(2,1)} %bitcast.2, s32[1,128]{1,0:T(1,128)} %bitcast.3), custom_call_target="tpu_custom_call" | custom-call | tf_op jit(solution)/shard_map/localized_covariance/pallas_call | solution.py:271
  164.7 1.3 copy.8

commit v4 on v3

--- a/solution.py
+++ b/solution.py
@@ -22,7 +22,7 @@
     quarter = levels // n_mem
     slots = active.shape[0]
     chunks = variables * halves
-    ahead = min(3, chunks)
+    ahead = min(6, chunks)
     side_by_side = 4 if n_col % 4 == 0 else 1
 
     def col_peer(step):
@@ -261,7 +261,7 @@
     members, variables, levels, width = ensemble.shape
     n_blocks, slots = tiles.shape[:2]
     per_device = members // n_col
-    halves = per_device // 2 if per_device % 4 == 0 else 2 - per_device % 2
+    halves = per_device
     group = per_device // halves
     chunks = variables * halves
     quarter = levels // n_mem

time: 166 us -> 169 us (1.018)
  Pallas kernels: 165 us -> 168 us
    pallas_call x1, Pallas kernels: 165 us -> 168 us  [on_device(): pl.pallas_call(functools.partial(kernel, n_mem, n_col, halves, float(memb...]
where the time goes in v4:
time: 169 us
  Pallas kernels  168 us (99%)
    pallas_call x1, Pallas kernels, on_device(): pl.pallas_call(functools.partial(kernel, n_mem, n_col, halves, float(memb...  168 us

profile of v4, /device:TPU:0, one launch (start us, length us, event | category | flops | bytes accessed | tf_op | source)
XLA Modules:
  0.0 168.9 jit_solution(14996311034217191626)
XLA Ops:
  0.0 167.6 %localized_covariance.1 = bf16[3,32,128]{2,1,0:T(8,128)(2,1)} custom-call(s32[8,8]{1,0:T(8,128)} %slot_block.1, bf16[64,3,128,128]{3,2,1,0:T(8,128)(2,1)} %ens.1, bf16[3,32,128]{2,1,0:T(8,128)(2,1)} %inc.1, bf16[3,128,128]{2,1,0:T(8,128)(2,1)} %root_in.1, bf16[8,1024,128]{2,1,0:T(8,128)(2,1)} %bitcast.2, s32[1,128]{1,0:T(1,128)} %bitcast.3), custom_call_target="tpu_custom_call" | custom-call | tf_op jit(solution)/shard_map/localized_covariance/pallas_call | solution.py:271
  167.6 1.3 copy.8

commit v5 on v3

--- a/solution.py
+++ b/solution.py
@@ -28,8 +28,22 @@
     def col_peer(step):
         return lax.rem(col + step, n_col)
 
-    def mem_peer(step):
-        return lax.rem(mem + step, n_mem)
+    lanes = 2 if n_col % 2 == 0 else 1
+    rows, planes = n_col // lanes, n_mem * lanes
+    lane, row = lax.rem(col, lanes), col // lanes
+    plane = mem * lanes + lane
+
+    def row_peer(step):
+        return lax.rem(row + step, rows)
+
+    def plane_peer(step):
+        return lax.rem(plane + step, planes)
+
+    def in_row(peer):
+        return {"col": peer * lanes + lane}
+
+    def in_plane(peer):
+        return {"mem": peer // lanes, "col": row * lanes + lax.rem(peer, lanes)}
 
     def each(low, high, body):
         def step(index, carry):
@@ -80,51 +94,53 @@
         each(1, n_col, lambda k: member_copy(chunk, far_first(k)).start())
 
     def inc_copy(step):
-        peer = col_peer(step)
-        return remote(inc, incr.at[mem, col], inc_send.at[peer], inc_recv.at[col], {"col": peer})
+        peer = row_peer(step)
+        return remote(inc, incr.at[plane, row], inc_send.at[peer], inc_recv.at[row], in_row(peer))
 
     def inc_arrival(step):
-        peer = col_peer(step)
-        return remote(inc, incr.at[mem, peer], inc_send.at[peer], inc_recv.at[peer], {"col": peer})
+        peer = row_peer(step)
+        return remote(inc, incr.at[plane, peer], inc_send.at[peer], inc_recv.at[peer], in_row(peer))
 
     def inc2_copy(step):
-        peer = mem_peer(step)
-        return remote(
-            incr.at[mem], incr.at[mem], inc2_send.at[peer], inc2_recv.at[mem], {"mem": peer}
+        peer = plane_peer(step)
+        return remote(
+            incr.at[plane], incr.at[plane], inc2_send.at[peer], inc2_recv.at[plane],
+            in_plane(peer),
         )
 
     def inc2_arrival(step):
-        peer = mem_peer(step)
-        return remote(
-            incr.at[peer], incr.at[peer], inc2_send.at[peer], inc2_recv.at[peer], {"mem": peer}
+        peer = plane_peer(step)
+        return remote(
+            incr.at[peer], incr.at[peer], inc2_send.at[peer], inc2_recv.at[peer],
+            in_plane(peer),
         )
 
     def part_copy(v, step):
-        peer = mem_peer(step)
-        return remote(
-            part_out.at[v, peer], part_in.at[v, mem],
-            part_send.at[v, peer], part_recv.at[v, mem], {"mem": peer},
+        peer = plane_peer(step)
+        return remote(
+            part_out.at[v, peer], part_in.at[v, plane],
+            part_send.at[v, peer], part_recv.at[v, plane], in_plane(peer),
         )
 
     def part_arrival(v, step):
-        peer = mem_peer(step)
+        peer = plane_peer(step)
         return remote(
             part_out.at[v, peer], part_in.at[v, peer],
-            part_send.at[v, peer], part_recv.at[v, peer], {"mem": peer},
+            part_send.at[v, peer], part_recv.at[v, peer], in_plane(peer),
         )
 
     def line_copy(v, step):
-        peer = col_peer(step)
-        return remote(
-            line_out.at[v, peer], line_in.at[v, col],
-            line_send.at[v, peer], line_recv.at[v, col], {"col": peer},
+        peer = row_peer(step)
+        return remote(
+            line_out.at[v, peer], line_in.at[v, row],
+            line_send.at[v, peer], line_recv.at[v, row], in_row(peer),
         )
 
     def line_arrival(v, step):
-        peer = col_peer(step)
+        peer = row_peer(step)
         return remote(
             line_out.at[v, peer], line_in.at[v, peer],
-            line_send.at[v, peer], line_recv.at[v, peer], {"col": peer},
+            line_send.at[v, peer], line_recv.at[v, peer], in_row(peer),
         )
 
     root_load = pltpu.make_async_copy(root_in, root, load_sem.at[0])
@@ -138,16 +154,16 @@
             barrier, inc=1, device_id={"col": col_peer(step)},
             device_id_type=pl.DeviceIdType.MESH,
         )
-    for step in range(1, n_mem):
+    for step in range(lanes, planes):
+        away = lax.rem(mem * lanes + step, planes)
         pl.semaphore_signal(
-            barrier, inc=1, device_id={"mem": mem_peer(step)},
-            device_id_type=pl.DeviceIdType.MESH,
-        )
-    pl.semaphore_wait(barrier, n_col + n_mem - 2)
-
-    each(1, n_col, lambda step: inc_copy(step).start())
+            barrier, inc=1, device_id=in_plane(away), device_id_type=pl.DeviceIdType.MESH
+        )
+    pl.semaphore_wait(barrier, n_col - 1 + planes - lanes)
+
+    each(1, rows, lambda step: inc_copy(step).start())
     each(0, ahead, send_chunk)
-    incr[mem, col] = inc[...]
+    incr[plane, row] = inc[...]
     reach_rows = jnp.broadcast_to(reach[...].astype(jnp.float32), (width, levels)).T
     for s in range(slots):
         active[s] = jnp.where(reach_rows > float(s), 1.0, 0.0).astype(jnp.bfloat16)
@@ -156,27 +172,27 @@
         root_t[v] = root[v].astype(jnp.float32).T.astype(jnp.bfloat16)
 
     def clear(v):
-        for p in range(n_mem):
+        for p in range(planes):
             total[v, p] = jnp.zeros(total.shape[2:], jnp.float32)
 
     each(0, variables, clear)
     tiles_load.wait()
-    each(1, n_col, lambda step: inc_arrival(step).wait_recv())
-    each(1, n_mem, lambda step: inc2_copy(step).start())
-    each(1, n_mem, lambda step: inc2_arrival(step).wait_recv())
+    each(1, rows, lambda step: inc_arrival(step).wait_recv())
+    each(1, planes, lambda step: inc2_copy(step).start())
+    each(1, planes, lambda step: inc2_arrival(step).wait_recv())
 
     def finish_levels(v):
-        each(1, n_mem, lambda step: part_arrival(v, step).wait_recv())
+        each(1, planes, lambda step: part_arrival(v, step).wait_recv())
 
         def block(b):
-            summed = total[v, mem, b]
-            for step in range(1, n_mem):
-                summed += part_in[v, mem_peer(step), b].astype(jnp.float32)
-            total[v, mem, b] = summed
+            summed = total[v, plane, b]
+            for step in range(1, planes):
+                summed += part_in[v, plane_peer(step), b].astype(jnp.float32)
+            total[v, plane, b] = summed
             line_out[v, b] = summed.astype(jnp.bfloat16)
 
-        each(0, n_col, block)
-        each(1, n_col, lambda step: line_copy(v, step).start())
+        each(0, rows, block)
+        each(1, rows, lambda step: line_copy(v, step).start())
 
     def chunk_step(chunk):
         v, half = chunk // halves, lax.rem(chunk, halves)
@@ -188,7 +204,9 @@
             send_chunk(chunk + ahead)
 
         def lift(b):
-            field = jnp.concatenate([incr[p, b, v] for p in range(n_mem)], 0).astype(jnp.float32)
+            field = jnp.concatenate(
+                [incr[p * lanes + lax.rem(b, lanes), b // lanes, v] for p in range(n_mem)], 0
+            ).astype(jnp.float32)
             weighted = jnp.concatenate(
                 [
                     (recv[chunk, b, i].astype(jnp.float32) * field).astype(jnp.bfloat16)
@@ -222,15 +240,15 @@
                     recv[chunk, r, i].astype(jnp.float32) * lowered[:, i * width:(i + 1) * width]
                 )
             for p in range(n_mem):
-                total[v, p, r] += summed[p * quarter:(p + 1) * quarter]
+                total[v, p * lanes + lax.rem(r, lanes), r // lanes] += summed[p * quarter:(p + 1) * quarter]
 
         together(spread)
 
         @pl.when(half == halves - 1)
         def _():
-            for p in range(n_mem):
+            for p in range(planes):
                 part_out[v, p] = total[v, p].astype(jnp.bfloat16)
-            each(1, n_mem, lambda step: part_copy(v, step).start())
+            each(1, planes, lambda step: part_copy(v, step).start())
 
         @pl.when((half == 0) & (v > 0))
         def _():
@@ -240,20 +258,20 @@
     finish_levels(variables - 1)
 
     for v in range(variables):
-        each(1, n_col, lambda step: line_arrival(v, step).wait_recv())
-        summed = total[v, mem, col]
-        for step in range(1, n_col):
-            summed += line_in[v, col_peer(step)].astype(jnp.float32)
+        each(1, rows, lambda step: line_arrival(v, step).wait_recv())
+        summed = total[v, plane, row]
+        for step in range(1, rows):
+            summed += line_in[v, row_peer(step)].astype(jnp.float32)
         out[v] = (summed / scale).astype(out.dtype)
 
-    each(1, n_col, lambda step: inc_copy(step).wait_send())
-    each(1, n_mem, lambda step: inc2_copy(step).wait_send())
+    each(1, rows, lambda step: inc_copy(step).wait_send())
+    each(1, planes, lambda step: inc2_copy(step).wait_send())
     each(0, chunks, lambda chunk: each(
         1, n_col, lambda step: member_copy(chunk, step).wait_send()))
     each(0, variables, lambda v: each(
-        1, n_mem, lambda step: part_copy(v, step).wait_send()))
+        1, planes, lambda step: part_copy(v, step).wait_send()))
     each(0, variables, lambda v: each(
-        1, n_col, lambda step: line_copy(v, step).wait_send()))
+        1, rows, lambda step: line_copy(v, step).wait_send()))
 
 
 def on_device(ensemble, increment, vert_root, tiles, tile_col, level_reach):
@@ -265,6 +283,8 @@
     group = per_device // halves
     chunks = variables * halves
     quarter = levels // n_mem
+    lanes = 2 if n_col % 2 == 0 else 1
+    rows, planes = n_col // lanes, n_mem * lanes
     dma = pltpu.SemaphoreType.DMA
     vmem = pl.BlockSpec(memory_space=pltpu.VMEM)
     bf16 = jnp.bfloat16
@@ -284,24 +304,24 @@
             pltpu.VMEM((slots, levels, width), bf16),
             dma((2,)),
             pltpu.VMEM((chunks, n_col, group, levels, width), bf16),
-            pltpu.VMEM((n_mem, n_col, variables, quarter, width), bf16),
+            pltpu.VMEM((planes, rows, variables, quarter, width), bf16),
             pltpu.VMEM((n_col, group, levels, width), bf16),
-            pltpu.VMEM((variables, n_mem, n_col, quarter, width), jnp.float32),
-            pltpu.VMEM((variables, n_mem, n_col, quarter, width), bf16),
-            pltpu.VMEM((variables, n_mem, n_col, quarter, width), bf16),
-            pltpu.VMEM((variables, n_col, quarter, width), bf16),
-            pltpu.VMEM((variables, n_col, quarter, width), bf16),
+            pltpu.VMEM((variables, planes, rows, quarter, width), jnp.float32),
+            pltpu.VMEM((variables, planes, rows, quarter, width), bf16),
+            pltpu.VMEM((variables, planes, rows, quarter, width), bf16),
+            pltpu.VMEM((variables, rows, quarter, width), bf16),
+            pltpu.VMEM((variables, rows, quarter, width), bf16),
             dma((chunks, n_col)),
             dma((chunks, n_col)),
             dma((chunks,)),
-            dma((n_col,)),
-            dma((n_col,)),
-            dma((n_mem,)),
-            dma((n_mem,)),
-            dma((variables, n_mem)),
-            dma((variables, n_mem)),
-            dma((variables, n_col)),
-            dma((variables, n_col)),
+            dma((rows,)),
+            dma((rows,)),
+            dma((planes,)),
+            dma((planes,)),
+            dma((variables, planes)),
+            dma((variables, planes)),
+            dma((variables, rows)),
+            dma((variables, rows)),
         ],
         compiler_params=pltpu.CompilerParams(
             collective_id=0, has_side_effects=True, vmem_limit_bytes=56 * 1024 * 1024

time: 166 us -> 163 us (0.982)
  Pallas kernels: 165 us -> 161 us
    pallas_call x1, Pallas kernels: 165 us -> 161 us  [on_device(): pl.pallas_call(functools.partial(kernel, n_mem, n_col, halves, float(memb...]
where the time goes in v5:
time: 163 us
  Pallas kernels  161 us (99%)
    pallas_call x1, Pallas kernels, on_device(): pl.pallas_call(functools.partial(kernel, n_mem, n_col, halves, float(memb...  161 us

profile of v5, /device:TPU:0, one launch (start us, length us, event | category | flops | bytes accessed | tf_op | source)
XLA Modules:
  0.0 162.7 jit_solution(17628592707260039095)
XLA Ops:
  0.0 161.4 %localized_covariance.1 = bf16[3,32,128]{2,1,0:T(8,128)(2,1)} custom-call(s32[8,8]{1,0:T(8,128)} %slot_block.1, bf16[64,3,128,128]{3,2,1,0:T(8,128)(2,1)} %ens.1, bf16[3,32,128]{2,1,0:T(8,128)(2,1)} %inc.1, bf16[3,128,128]{2,1,0:T(8,128)(2,1)} %root_in.1, bf16[8,1024,128]{2,1,0:T(8,128)(2,1)} %bitcast.2, s32[1,128]{1,0:T(1,128)} %bitcast.3), custom_call_target="tpu_custom_call" | custom-call | tf_op jit(solution)/shard_map/localized_covariance/pallas_call | solution.py:291
  161.4 1.3 copy.8

commit v6 on v5

--- a/solution.py
+++ b/solution.py
@@ -9,7 +9,7 @@
 
 
 def kernel(
-    n_mem, n_col, halves, scale,
+    n_mem, n_col, halves, parts, scale,
     slot_block, ens, inc, root_in, tiles_in, reach, out,
     root, root_t, tiles, active, load_sem, recv, incr, grid, total, part_out, part_in, line_out, line_in,
     send_sem, recv_sem, own_sem, inc_send, inc_recv, inc2_send, inc2_recv,
@@ -32,6 +32,7 @@
     rows, planes = n_col // lanes, n_mem * lanes
     lane, row = lax.rem(col, lanes), col // lanes
     plane = mem * lanes + lane
+    span = rows // parts
 
     def row_peer(step):
         return lax.rem(row + step, rows)
@@ -51,11 +52,11 @@
             return carry
         lax.fori_loop(low, high, step, 0)
 
-    def together(body):
+    def together(low, high, body):
         def step(index):
             for k in range(side_by_side):
                 body(index * side_by_side + k)
-        each(0, n_col // side_by_side, step)
+        each(low, high, step)
 
     def remote(src, dst, send, receive, peer):
         return pltpu.make_async_remote_copy(
@@ -115,18 +116,20 @@
             in_plane(peer),
         )
 
-    def part_copy(v, step):
-        peer = plane_peer(step)
-        return remote(
-            part_out.at[v, peer], part_in.at[v, plane],
-            part_send.at[v, peer], part_recv.at[v, plane], in_plane(peer),
-        )
-
-    def part_arrival(v, step):
-        peer = plane_peer(step)
-        return remote(
-            part_out.at[v, peer], part_in.at[v, peer],
-            part_send.at[v, peer], part_recv.at[v, peer], in_plane(peer),
+    def part_copy(v, part, step):
+        peer, blocks = plane_peer(step), pl.ds(part * span, span)
+        return remote(
+            part_out.at[v, peer, blocks], part_in.at[v, plane, blocks],
+            part_send.at[v * parts + part, peer], part_recv.at[v * parts + part, plane],
+            in_plane(peer),
+        )
+
+    def part_arrival(v, part, step):
+        peer, blocks = plane_peer(step), pl.ds(part * span, span)
+        return remote(
+            part_out.at[v, peer, blocks], part_in.at[v, peer, blocks],
+            part_send.at[v * parts + part, peer], part_recv.at[v * parts + part, peer],
+            in_plane(peer),
         )
 
     def line_copy(v, step):
@@ -182,7 +185,8 @@
     each(1, planes, lambda step: inc2_arrival(step).wait_recv())
 
     def finish_levels(v):
-        each(1, planes, lambda step: part_arrival(v, step).wait_recv())
+        for part in range(parts):
+            each(1, planes, lambda step: part_arrival(v, part, step).wait_recv())
 
         def block(b):
             summed = total[v, plane, b]
@@ -197,11 +201,6 @@
     def chunk_step(chunk):
         v, half = chunk // halves, lax.rem(chunk, halves)
         own_copy(chunk).wait()
-        each(1, n_col, lambda step: member_arrival(chunk, step).wait_recv())
-
-        @pl.when(chunk + ahead < chunks)
-        def _():
-            send_chunk(chunk + ahead)
 
         def lift(b):
             field = jnp.concatenate(
@@ -220,7 +219,22 @@
             for i in range(group):
                 grid[b, i] = lifted[:, i * width:(i + 1) * width]
 
-        together(lift)
+        def lift_group(index):
+            order = [index * side_by_side + k for k in range(side_by_side)]
+            for place in order:
+
+                @pl.when(place > 0)
+                def _():
+                    member_arrival(chunk, far_first(n_col - place)).wait_recv()
+
+            for place in order:
+                lift(col_peer(far_first(n_col - place)))
+
+        each(0, n_col // side_by_side, lift_group)
+
+        @pl.when(chunk + ahead < chunks)
+        def _():
+            send_chunk(chunk + ahead)
 
         def spread(r):
             picked = jnp.concatenate(
@@ -242,13 +256,18 @@
             for p in range(n_mem):
                 total[v, p * lanes + lax.rem(r, lanes), r // lanes] += summed[p * quarter:(p + 1) * quarter]
 
-        together(spread)
-
-        @pl.when(half == halves - 1)
-        def _():
-            for p in range(planes):
-                part_out[v, p] = total[v, p].astype(jnp.bfloat16)
-            each(1, planes, lambda step: part_copy(v, step).start())
+        def spread_part(part):
+            groups = n_col // side_by_side // parts
+            together(part * groups, (part + 1) * groups, spread)
+
+            @pl.when(half == halves - 1)
+            def _():
+                blocks = pl.ds(part * span, span)
+                for p in range(planes):
+                    part_out[v, p, blocks] = total[v, p, blocks].astype(jnp.bfloat16)
+                each(1, planes, lambda step: part_copy(v, part, step).start())
+
+        each(0, parts, spread_part)
 
         @pl.when((half == 0) & (v > 0))
         def _():
@@ -269,7 +288,7 @@
     each(0, chunks, lambda chunk: each(
         1, n_col, lambda step: member_copy(chunk, step).wait_send()))
     each(0, variables, lambda v: each(
-        1, planes, lambda step: part_copy(v, step).wait_send()))
+        1, planes, lambda step: [part_copy(v, part, step).wait_send() for part in range(parts)]))
     each(0, variables, lambda v: each(
         1, rows, lambda step: line_copy(v, step).wait_send()))
 
@@ -285,11 +304,12 @@
     quarter = levels // n_mem
     lanes = 2 if n_col % 2 == 0 else 1
     rows, planes = n_col // lanes, n_mem * lanes
+    parts = 2 if n_col % 8 == 0 else 1
     dma = pltpu.SemaphoreType.DMA
     vmem = pl.BlockSpec(memory_space=pltpu.VMEM)
     bf16 = jnp.bfloat16
     return pl.pallas_call(
-        functools.partial(kernel, n_mem, n_col, halves, float(members * n_mem - 1)),
+        functools.partial(kernel, n_mem, n_col, halves, parts, float(members * n_mem - 1)),
         out_shape=jax.ShapeDtypeStruct(increment.shape, bf16),
         in_specs=[
             pl.BlockSpec(memory_space=pltpu.SMEM),
@@ -318,8 +338,8 @@
             dma((rows,)),
             dma((planes,)),
             dma((planes,)),
-            dma((variables, planes)),
-            dma((variables, planes)),
+            dma((variables * parts, planes)),
+            dma((variables * parts, planes)),
             dma((variables, rows)),
             dma((variables, rows)),
         ],

time: 163 us -> 163 us (level)
  no operation moved by 1% of the time
where the time goes in v6:
time: 163 us
  Pallas kernels  162 us (99%)
    pallas_call x1, Pallas kernels, on_device(): pl.pallas_call(functools.partial(kernel, n_mem, n_col, halves, parts, flo...  162 us

profile of v6, /device:TPU:0, one launch (start us, length us, event | category | flops | bytes accessed | tf_op | source)
XLA Modules:
  0.0 163.1 jit_solution(14799546276387979138)
XLA Ops:
  0.0 161.7 %localized_covariance.1 = bf16[3,32,128]{2,1,0:T(8,128)(2,1)} custom-call(s32[8,8]{1,0:T(8,128)} %slot_block.1, bf16[64,3,128,128]{3,2,1,0:T(8,128)(2,1)} %ens.1, bf16[3,32,128]{2,1,0:T(8,128)(2,1)} %inc.1, bf16[3,128,128]{2,1,0:T(8,128)(2,1)} %root_in.1, bf16[8,1024,128]{2,1,0:T(8,128)(2,1)} %bitcast.2, s32[1,128]{1,0:T(1,128)} %bitcast.3), custom_call_target="tpu_custom_call" | custom-call | tf_op jit(solution)/shard_map/localized_covariance/pallas_call | solution.py:311
  161.7 1.3 copy.8

commit v7 on v6

--- a/solution.py
+++ b/solution.py
@@ -22,7 +22,7 @@
     quarter = levels // n_mem
     slots = active.shape[0]
     chunks = variables * halves
-    ahead = min(3, chunks)
+    ahead = min(2, chunks)
     side_by_side = 4 if n_col % 4 == 0 else 1
 
     def col_peer(step):

time: 163 us -> 163 us (level)
  no operation moved by 1% of the time
where the time goes in v7:
time: 163 us
  Pallas kernels  162 us (99%)
    pallas_call x1, Pallas kernels, on_device(): pl.pallas_call(functools.partial(kernel, n_mem, n_col, halves, parts, flo...  162 us

profile of v7, /device:TPU:0, one launch (start us, length us, event | category | flops | bytes accessed | tf_op | source)
XLA Modules:
  0.0 163.2 jit_solution(15413773071834626424)
XLA Ops:
  0.0 161.8 %localized_covariance.1 = bf16[3,32,128]{2,1,0:T(8,128)(2,1)} custom-call(s32[8,8]{1,0:T(8,128)} %slot_block.1, bf16[64,3,128,128]{3,2,1,0:T(8,128)(2,1)} %ens.1, bf16[3,32,128]{2,1,0:T(8,128)(2,1)} %inc.1, bf16[3,128,128]{2,1,0:T(8,128)(2,1)} %root_in.1, bf16[8,1024,128]{2,1,0:T(8,128)(2,1)} %bitcast.2, s32[1,128]{1,0:T(1,128)} %bitcast.3), custom_call_target="tpu_custom_call" | custom-call | tf_op jit(solution)/shard_map/localized_covariance/pallas_call | solution.py:311
  161.8 1.3 copy.8

commit v8 on v7

--- a/solution.py
+++ b/solution.py
@@ -298,7 +298,7 @@
     members, variables, levels, width = ensemble.shape
     n_blocks, slots = tiles.shape[:2]
     per_device = members // n_col
-    halves = per_device // 2 if per_device % 4 == 0 else 2 - per_device % 2
+    halves = 2 - per_device % 2
     group = per_device // halves
     chunks = variables * halves
     quarter = levels // n_mem

time: 163 us -> 165 us (1.012)
  no operation moved by 1% of the time
where the time goes in v8:
time: 165 us
  Pallas kernels  163 us (99%)
    pallas_call x1, Pallas kernels, on_device(): pl.pallas_call(functools.partial(kernel, n_mem, n_col, halves, parts, flo...  163 us

profile of v8, /device:TPU:0, one launch (start us, length us, event | category | flops | bytes accessed | tf_op | source)
XLA Modules:
  0.0 164.6 jit_solution(11883841210304198675)
XLA Ops:
  0.0 163.2 %localized_covariance.1 = bf16[3,32,128]{2,1,0:T(8,128)(2,1)} custom-call(s32[8,8]{1,0:T(8,128)} %slot_block.1, bf16[64,3,128,128]{3,2,1,0:T(8,128)(2,1)} %ens.1, bf16[3,32,128]{2,1,0:T(8,128)(2,1)} %inc.1, bf16[3,128,128]{2,1,0:T(8,128)(2,1)} %root_in.1, bf16[8,1024,128]{2,1,0:T(8,128)(2,1)} %bitcast.2, s32[1,128]{1,0:T(1,128)} %bitcast.3), custom_call_target="tpu_custom_call" | custom-call | tf_op jit(solution)/shard_map/localized_covariance/pallas_call | solution.py:311
  163.2 1.3 copy.8
